TPU v7x, 256 devices: a whole 4x4x8 slice. The times are simulated.
256 devices in a mesh: row: 32 (over y, z), col: 8 (over x, core).
Axes of the slice: x: 4, y: 4, z: 8, core: 2. Of those that a mesh axis runs over, the one named last changes fastest.
Arguments:
- image_rows: bfloat16 [24576, 1024], P('row', 'col'), may hold values from -16 to 16, as said below
- text_rows: bfloat16 [24576, 1024], P('col', 'row'), may hold values from -16 to 16, as said below
Outputs:
- loss: float32 [], replicated
- picture_derivative: float32 [24576, 1024], P('row', 'col')
- text_grad: float32 [24576, 1024], P('col', 'row')
Inputs may be any that keep to these rules, and one draw needn't show every extreme that they name: `image_rows`: image embeddings, of order one per entry. `text_rows`: text embeddings, of order one per entry.
All inputs are finite; a program needn't handle non-finite values.
Results may differ from a plain program's by a relative error of at most 0.0018.
Values may be sent and summed in bfloat16 or wider, within the bound.
A program may use at most 128 MiB of HBM per device.

v0:
```python
import math

import jax
import jax.numpy as jnp
from jax import lax
from jax.sharding import PartitionSpec as P

VECTOR_DIMENSION = 1024


sharpness_divisor = 0.25


def shards(image_rows, text_rows):
    similarity_gain = 1.0 / (sharpness_divisor * math.sqrt(VECTOR_DIMENSION))
    image_block = lax.all_gather(image_rows, "col", axis=1, tiled=True)
    img_count = image_block.shape[0]
    txt_count = text_rows.shape[0]
    batch_count_total = img_count * lax.axis_size("row")
    text_block = lax.all_gather(text_rows, "row", axis=1, tiled=True)
    logits = (
        jnp.dot(image_block, text_block.T, preferred_element_type=jnp.float32) * similarity_gain
    )
    row_ids = lax.axis_index("row") * img_count + jnp.arange(img_count, dtype=jnp.int32)
    col_ids = lax.axis_index("col") * txt_count + jnp.arange(txt_count, dtype=jnp.int32)
    diag_mask = row_ids[:, None] == col_ids[None, :]
    masked = jnp.where(diag_mask, logits, 0.0)
    row_pos_local = jnp.sum(masked, axis=1)
    col_pos_local = jnp.sum(masked, axis=0)
    row_top = lax.pmax(jnp.max(logits, axis=1), "col")
    col_top = lax.pmax(jnp.max(logits, axis=0), "row")
    row_sum, row_pos = lax.psum(
        (jnp.sum(jnp.exp(logits - row_top[:, None]), axis=1), row_pos_local), "col"
    )
    col_sum, col_pos = lax.psum(
        (jnp.sum(jnp.exp(logits - col_top[None, :]), axis=0), col_pos_local), "row"
    )
    row_lse = row_top + jnp.log(row_sum)
    col_lse = col_top + jnp.log(col_sum)
    row_term = jnp.where(lax.axis_index("col") == 0, jnp.sum(row_lse - row_pos), 0.0)
    col_term = jnp.where(lax.axis_index("row") == 0, jnp.sum(col_lse - col_pos), 0.0)
    loss_sum = lax.psum(row_term + col_term, ("row", "col"))
    loss = loss_sum / (2.0 * batch_count_total)
    weights = (
        jnp.exp(logits - row_lse[:, None])
        + jnp.exp(logits - col_lse[None, :])
        - 2.0 * diag_mask.astype(jnp.float32)
    ).astype(jnp.bfloat16)
    picture_addend = jnp.dot(weights, text_block, preferred_element_type=jnp.float32)
    caption_addend = jnp.dot(weights.T, image_block, preferred_element_type=jnp.float32)
    factor = similarity_gain / (2.0 * batch_count_total)
    picture_derivative = factor * lax.psum_scatter(
        picture_addend, "col", scatter_dimension=1, tiled=True
    )
    text_sum_reduced = lax.psum_scatter(caption_addend, "row", scatter_dimension=1, tiled=True)
    text_grad = factor * text_sum_reduced
    return (loss, picture_derivative, text_grad)


def solution(mesh):
    placed = (P("row", "col"), P("col", "row"))
    return jax.shard_map(
        shards,
        mesh=mesh,
        in_specs=placed,
        out_specs=(P(), P("row", "col"), P("col", "row")),
        check_vma=False,
    )
```

profile of v0, /device:TPU:30, one launch (start us, length us, event | category | flops | bytes accessed | tf_op | source)
XLA Modules:
  0.0 754.9 jit_solution(14715106705536715429)
XLA Ops:
  7.2 0.0 all-gather.3.cloned.1.call-start
  7.2 0.7 all-gather.3.cloned.1.call-update
  7.9 0.0 all-gather.5.cloned.1.call-start
  7.9 0.7 all-gather.5.cloned.1.call-update
  8.6 0.0 reduce-scatter.3.cloned.1.call-start
  8.7 30.8 %all-gather.3.cloned.1.call-done = bf16[768,1024]{1,0:T(8,128)(2,1)} async-done(((bf16[768,128]{1,0:T(8,128)(2,1)}), bf16[768,1024]{1,0:T(8,128)(2,1)}) %all-gather.3.cloned.1.call-update) | async-done | bytes 1572880 | tf_op jit(solution)/shard_map/all_gather | solution.py:16
  39.5 91.1 %all-gather.5.cloned.1.call-done = bf16[3072,1024]{0,1:T(8,128)(2,1)} async-done(((bf16[3072,32]{0,1:T(8,128)(2,1)}), bf16[3072,1024]{0,1:T(8,128)(2,1)}) %all-gather.5.cloned.1.call-update) | async-done | bytes 6291472 | tf_op jit(solution)/shard_map/all_gather | solution.py:20
  130.6 9.9 %multiply_reduce_fusion.1 = (f32[768]{0:T(1024)S(1)}, f32[768,3072]{1,0:T(8,128)}) fusion(bf16[768,1024]{1,0:T(8,128)(2,1)} %all-gather.3.cloned.1.call-done, bf16[3072,1024]{0,1:T(8,128)(2,1)} %all-gather.5.cloned.1.call-done), kind=kOutput, calls=%fused_computation.9 | convolution fusion | flops 4836555776 | bytes 17304576 | tf_op jit(solution)/shard_map/dot_general | solution.py:22
  140.5 10.0 %pmax.14 = f32[768]{0:T(1024)S(1)} all-reduce(f32[768]{0:T(1024)S(1)} %get-tuple-element.15), channel_id=1, replica_groups=mesh['row'=32,'col'=8] {'col'}, use_global_device_ids=true, to_apply=%region_1.2 | all-reduce | flops 768 | bytes 6144 | tf_op jit(solution)/shard_map/pmax | solution.py:30
  150.5 7.0 fusion.2
  157.5 128.4 %pmax.15 = f32[3072]{0:T(1024)S(1)} all-reduce(f32[3072]{0:T(1024)S(1)} %get-tuple-element.6), channel_id=1, replica_groups=mesh['row'=32,'col'=8] {'row'}, use_global_device_ids=true, to_apply=%region_8.9 | all-reduce | flops 3072 | bytes 24576 | tf_op jit(solution)/shard_map/pmax | solution.py:31
  285.9 5.2 exponential_reduce_fusion
  291.2 12.8 %all-reduce.1 = (f32[768]{0:T(1024)S(1)}, f32[768]{0:T(1024)S(1)}) all-reduce(f32[768]{0:T(1024)S(1)} %get-tuple-element.5, f32[768]{0:T(1024)S(1)} %get-tuple-element.4), channel_id=1, replica_groups=mesh['row'=32,'col'=8] {'col'}, use_global_device_ids=true, to_apply=%region_3.4 | all-reduce | flops 1536 | bytes 12288 | tf_op jit(solution)/shard_map/psum | solution.py:32
  304.0 0.6 subtract_reduce_fusion.1
  304.6 137.7 %all-reduce = (f32[3072]{0:T(1024)S(1)}, f32[3072]{0:T(1024)S(1)}) all-reduce(f32[3072]{0:T(1024)S(1)} %exponential_reduce_fusion, f32[3072]{0:T(1024)S(1)} %get-tuple-element.3), channel_id=1, replica_groups=mesh['row'=32,'col'=8] {'row'}, use_global_device_ids=true, to_apply=%region_10.11 | all-reduce | flops 6144 | bytes 49152 | tf_op jit(solution)/shard_map/psum | solution.py:35
  442.3 0.6 subtract_reduce_fusion
  442.9 6.7 fusion.1
  449.6 0.0 copy-start
  449.6 2.1 copy-done
  451.7 0.0 copy-start.1
  451.7 8.5 %fusion.4 = f32[768,1024]{1,0:T(8,128)} fusion(bf16[768,3072]{1,0:T(8,128)(2,1)S(1)} %fusion.1, bf16[3072,1024]{0,1:T(8,128)(2,1)} %all-gather.5.cloned.1.call-done), kind=kOutput, calls=%fused_computation.18 | convolution fusion | flops 4831838208 | bytes 14155776 | tf_op jit(solution)/shard_map/dot_general | solution.py:49
  460.2 0.0 reduce-scatter.3.cloned.1.call-update
  460.2 0.2 reduce-scatter.5.cloned.1.call-start
  460.4 0.0 copy-done.1
  460.4 10.4 %fusion.5 = f32[3072,1024]{0,1:T(8,128)} fusion(bf16[768,3072]{1,0:T(8,128)(2,1)} %copy-done, bf16[768,1024]{1,0:T(8,128)(2,1)S(1)} %copy-done.1), kind=kOutput, calls=%fused_computation.19 | convolution fusion | flops 4831838208 | bytes 18874368 | tf_op jit(solution)/shard_map/dot_general | solution.py:50
  470.8 0.0 reduce-scatter.5.cloned.1.call-update
  472.1 85.8 %psum.39 = f32[]{:T(128)} all-reduce(f32[]{:T(128)S(6)} %add.52), channel_id=1, replica_groups=mesh['row'=32,'col'=8] {'row','col'}, use_global_device_ids=true, to_apply=%region_14.15 | all-reduce | flops 1 | bytes 8 | tf_op jit(solution)/shard_map/psum | solution.py:42
  558.6 0.0 reduce-scatter.3.cloned.1.call-done
  558.6 1.8 broadcast_multiply_fusion.1
  560.4 185.0 %reduce-scatter.5.cloned.1.call-done = f32[3072,32]{0,1:T(8,128)} async-done(((f32[3072,1024]{0,1:T(8,128)}), f32[3072,32]{0,1:T(8,128)}) %reduce-scatter.5.cloned.1.call-update) | async-done | bytes 393232 | tf_op jit(solution)/shard_map/reduce_scatter | solution.py:55
  745.4 1.8 broadcast_multiply_fusion
  (2 shorter events, 0.0 us)
Async XLA Ops:
  7.2 32.4 %all-gather.3.cloned.1.call-start = ((), (), s32[]{:S(2)}) async-start(), calls=%async_computation.2 | async-start | bytes 1769472 | tf_op jit(solution)/shard_map/all_gather | solution.py:16
  7.9 122.7 %all-gather.5.cloned.1.call-start = ((), (), s32[]{:S(2)}) async-start(), calls=%async_computation.3 | async-start | bytes 6488064 | tf_op jit(solution)/shard_map/all_gather | solution.py:20
  8.6 550.0 %reduce-scatter.3.cloned.1.call-start = ((), (), s32[]{:S(2)}) async-start(), calls=%async_computation.4 | async-start | bytes 3538944 | tf_op jit(solution)/shard_map/reduce_scatter | solution.py:52
  449.6 2.1 copy-start
  451.7 8.7 %copy-start.1 = (bf16[768,1024]{1,0:T(8,128)(2,1)S(1)}, bf16[768,1024]{1,0:T(8,128)(2,1)}, u32[]{:S(2)}) copy-start(bf16[768,1024]{1,0:T(8,128)(2,1)} %all-gather.3.cloned.1.call-done) | copy-start | bytes 4718596
  460.2 285.3 %reduce-scatter.5.cloned.1.call-start = ((), (), s32[]{:S(2)}) async-start(), calls=%async_computation.5 | async-start | bytes 12976128 | tf_op jit(solution)/shard_map/reduce_scatter | solution.py:55
Sparse Core Ops, SparseCore 0:
  9.8 29.6 all-gather.2
  42.1 88.4 all-gather.4
  460.3 42.5 reduce-scatter.2
  506.9 238.4 reduce-scatter.4
where the time goes:
time: 757 us; the launch traced here: 755 us
  blocking collectives  375 us (50%)
  waiting for transfers between devices  308 us (41%)
  matrix products  28.8 us (4%)
  other arithmetic  23.7 us (3%)
  between operations  16.9 us (2%)
    reduce_scatter x1, waiting for transfers between devices, shards(): lax.psum_scatter(caption_addend, 'row', scatter_dimension=1, tiled=True)  185 us
    psum x1, blocking collectives, shards(): lax.psum((jnp.sum(jnp.exp(logits - col_top[None, :]), axis=0), col_pos_lo...  138 us
    pmax x1, blocking collectives, shards(): col_top = lax.pmax(jnp.max(logits, axis=0), 'row')  128 us
    all_gather x1, waiting for transfers between devices, shards(): text_block = lax.all_gather(text_rows, 'row', axis=1, tiled=True)  91.1 us
    psum x1, blocking collectives, shards(): loss_sum = lax.psum(row_term + col_term, ('row', 'col'))  85.8 us
    all_gather x1, waiting for transfers between devices, shards(): image_block = lax.all_gather(image_rows, 'col', axis=1, tiled=True)  30.8 us
  transfers between devices with their start and end apart: 4, of which 3 were waited for; matrix products, arithmetic and copies ran while one was open for 2% of the time, Pallas kernels for 0%

commit v1 on v0

v1 whole, which is shorter than its diff:
```python
import math

import jax
import jax.numpy as jnp
from jax import lax
from jax.experimental import pallas as pl
from jax.experimental.pallas import tpu as pltpu
from jax.sharding import PartitionSpec as P

MESH = pl.DeviceIdType.MESH
LOG2E = 1.4426950408889634
SHARPNESS = 0.25
SUM_TYPE = jnp.float32

PARTS = ((0, 896, 512, "P"), (896, 640, 256, "Q"))
OFFSETS_Z = (4, 3, 5, 2, 6, 1, 7, 0)
OFFSETS_X = (2, 1, 3, 0)


def interleave(*streams):
    streams = list(streams)
    while streams:
        for stream in list(streams):
            try:
                next(stream)
            except StopIteration:
                streams.remove(stream)


def kernel(
    img_raw, txt_raw,
    loss_out, img_out, txt_out,
    img, imgt, txt, logits, w, tg, ig,
    row_m, row_s, col_m, col_s, row_st, col_st, row_lse_b, loss_r, loss_c,
    land_py, land_pz, land_qz, land_qy, land_c, land_x1, land_x2, land_xp, fin, land_o,
    send, recv, local,
):
    half = txt_raw.shape[1] // 2
    rows_own, feat_own = img_raw.shape
    rows = 2 * rows_own
    dim = img.shape[1]
    scale2 = LOG2E / (SHARPNESS * math.sqrt(dim))
    batch = rows * 16
    factor = 1.0 / (SHARPNESS * math.sqrt(dim)) / (2.0 * batch)

    row_id, col_id = lax.axis_index("row"), lax.axis_index("col")
    y, z = row_id // 8, row_id % 8
    x, c = col_id // 2, col_id % 2
    t, a = y // 2, y % 2

    def dev(dx=None, dy=None, dz=None, dc=None):
        dx = x if dx is None else dx
        dy = y if dy is None else dy
        dz = z if dz is None else dz
        dc = c if dc is None else dc
        return (dy * 8 + dz, dx * 2 + dc)

    y_mate = 2 * t + 1 - a
    y_part = 3 - y
    core_mate = dev(dc=1 - c)
    mate = dev(dy=y_mate)
    partner = dev(dy=y_part)
    z_next = {1: dev(dz=(z + 1) % 8), -1: dev(dz=(z + 7) % 8)}
    x_next = {1: dev(dx=(x + 1) % 4), -1: dev(dx=(x + 3) % 4)}

    def slot_of(yv, tv):
        h = (yv // 2 + tv) % 2
        return 2 * ((yv + h) % 2) + h

    g_row = (x * 2 + c) * 2 + t
    g_col = a * 8 + z

    def row_peer(k):
        g = (g_row + k) % 16
        tt = g % 2
        return dev(dx=g // 4, dc=(g // 2) % 2, dy=jnp.where(tt == t, y, 3 - y))

    def col_peer(k):
        g = (g_col + k) % 16
        return dev(dy=2 * t + g // 8, dz=g % 8)

    barrier = pltpu.get_barrier_semaphore()

    def greet(k, _):
        pl.semaphore_signal(barrier, inc=1, device_id=row_peer(k), device_id_type=MESH)
        pl.semaphore_signal(barrier, inc=1, device_id=col_peer(k), device_id_type=MESH)
        return 0

    lax.fori_loop(1, 16, greet, 0)
    pl.semaphore_wait(barrier, 30)

    count = [0]
    unsent = []

    def message(src, dst, device, start=True):
        k = count[0]
        count[0] += 1
        copy = pltpu.make_async_remote_copy(
            src_ref=src, dst_ref=dst, send_sem=send.at[k], recv_sem=recv.at[k],
            device_id=device, device_id_type=MESH,
        )
        if start:
            copy.start()
            unsent.append(copy)
        return copy

    def lanes(start, size):
        return pl.ds(pl.multiple_of(start, 128), size)

    def block(b):
        return pl.ds(pl.multiple_of(b * rows_own, rows_own), rows_own)

    def img_piece(xv, b, tv=t):
        return img.at[block(b), lanes(slot_of(xv, tv) * 256 + c * 128, 128)]

    def txt_unit(av, zv, c0, n):
        return txt.at[av, :, zv, :, pl.ds(c0, n)]

    same = t == c
    copy_img = pltpu.make_async_copy(img_raw, img_piece(x, t), local.at[0])
    copy_img.start()
    copy_txt = pltpu.make_async_copy(
        txt_raw.at[:, lanes(c * half, half)], txt.at[a, 0, z], local.at[1]
    )
    swap_own = message(txt_raw.at[:, lanes((1 - c) * half, half)], txt.at[a, 0, z], core_mate, start=False)
    k = count[0]
    count[0] += 2
    swap_far = [
        pltpu.make_async_remote_copy(
            src_ref=txt_raw.at[:, pl.ds(q * half, half)], dst_ref=txt.at[1 - a, 1, z],
            send_sem=send.at[k + q], recv_sem=recv.at[k],
            device_id=dev(dy=y_part, dc=q), device_id_type=MESH,
        )
        for q in range(2)
    ]
    swap_in = pltpu.make_async_remote_copy(
        src_ref=txt.at[a, 1, z], dst_ref=txt.at[a, 1, z], send_sem=send.at[k], recv_sem=recv.at[k],
        device_id=partner, device_id_type=MESH,
    )

    @pl.when(same)
    def _():
        swap_own.start()
        copy_txt.start()

    @pl.when(jnp.logical_not(same))
    def _():
        swap_far[0].start()
        swap_far[1].start()

    def gather_img():
        to_partner = message(img_raw, img_piece(x, t, 1 - t), partner)
        own = {d: message(img_raw, img_piece(x, t), x_next[d]) for d in (1, -1)}
        cores = [message(img_raw, img_piece(x, t), core_mate)]
        yield
        to_partner.wait_recv()
        other = {d: message(img_piece(x, 1 - t), img_piece(x, 1 - t), x_next[d]) for d in (1, -1)}
        cores.append(message(img_piece(x, 1 - t), img_piece(x, 1 - t), core_mate))
        yield
        xv = {1: (x + 3) % 4, -1: (x + 1) % 4}
        own[1].wait_recv()
        piece = img_piece(xv[1], t)
        far = {1: message(piece, piece, x_next[1])}
        cores.append(message(piece, piece, core_mate))
        own[-1].wait_recv()
        piece = img_piece(xv[-1], t)
        cores.append(message(piece, piece, core_mate))
        yield
        other[-1].wait_recv()
        piece = img_piece(xv[-1], 1 - t)
        far[-1] = message(piece, piece, x_next[-1])
        cores.append(message(piece, piece, core_mate))
        other[1].wait_recv()
        piece = img_piece(xv[1], 1 - t)
        cores.append(message(piece, piece, core_mate))
        yield
        xo = (x + 2) % 4
        far[1].wait_recv()
        cores.append(message(img_piece(xo, t), img_piece(xo, t), core_mate))
        yield
        far[-1].wait_recv()
        cores.append(message(img_piece(xo, 1 - t), img_piece(xo, 1 - t), core_mate))
        yield
        for copy in cores:
            copy.wait_recv()

    def gather_p(c0, n, n1):
        whole = lambda zv: txt_unit(a, zv, c0, n)
        halves = {1: (c0, n1), -1: (c0 + n1, n - n1)}
        ring = {d: message(whole(z), whole(z), z_next[d]) for d in (1, -1)}
        to_mate = [message(whole(z), whole(z), mate)]
        yield
        for hop in (1, 2, 3):
            onward = {}
            for d in (1, -1):
                ring[d].wait_recv()
                zv = (z - d * hop) % 8 if d == 1 else (z + hop) % 8
                unit = whole(zv) if hop < 3 else txt_unit(a, zv, *halves[d])
                onward[d] = message(unit, unit, z_next[d])
                to_mate.append(message(whole(zv), whole(zv), mate))
            ring = onward
            yield
        for d in (1, -1):
            ring[d].wait_recv()
        zv = (z + 4) % 8
        to_mate.append(message(whole(zv), whole(zv), mate))
        yield
        for copy in to_mate:
            copy.wait_recv()

    def gather_q(c0, n, n1):
        halves = {1: (c0, n1), -1: (c0 + n1, n - n1)}
        own = txt_unit(a, z, c0, n)
        rings = {(0, d): message(own, own, z_next[d]) for d in (1, -1)}
        to_mate = message(own, own, mate)
        yield
        to_mate.wait_recv()
        other = txt_unit(1 - a, z, c0, n)
        rings.update({(1, d): message(other, other, z_next[d]) for d in (1, -1)})
        yield
        for hop in (1, 2, 3):
            for which in (0, 1):
                for d in (1, -1):
                    rings[which, d].wait_recv()
                    zv = (z + 8 - d * hop) % 8
                    av = a if which == 0 else 1 - a
                    unit = txt_unit(av, zv, *((c0, n) if hop < 3 else halves[d]))
                    rings[which, d] = message(unit, unit, z_next[d])
                yield
        for copy in rings.values():
            copy.wait_recv()

    image_stream = gather_img()
    next(image_stream)

    @pl.when(same)
    def _():
        copy_txt.wait()

    @pl.when(jnp.logical_not(same))
    def _():
        swap_own.wait_recv()

    swap_in.wait_recv()
    copy_img.wait()
    streams = [image_stream]
    for c0, n, n1, kind in PARTS:
        streams.append((gather_p if kind == "P" else gather_q)(c0, n, n1))
    interleave(*streams)

    row_m[...] = jnp.full_like(row_m, -1e30)
    row_s[...] = jnp.zeros_like(row_s)
    col_m[...] = jnp.full_like(col_m, -1e30)
    col_s[...] = jnp.zeros_like(col_s)
    RB, CB = 256, 512

    def transpose_step(i, _):
        r = pl.ds(pl.multiple_of(i * RB, RB), RB)
        for s in range(4):
            imgt[s // 2, s % 2, :, r] = img[r, s * 256:(s + 1) * 256].T
        return 0

    lax.fori_loop(0, rows // RB, transpose_step, 0)

    def logits_step(i, _):
        r = pl.ds(pl.multiple_of((i % (rows // RB)) * RB, RB), RB)
        cc = lanes((i // (rows // RB)) * CB, CB)
        tv = txt[:, :, :, :, cc].reshape(dim, CB)
        v = jnp.dot(img[r, :], tv, preferred_element_type=jnp.float32) * scale2
        logits[r, cc] = v
        parts = [v[:, j * 128:(j + 1) * 128] for j in range(CB // 128)]
        m_old = row_m[r, :]
        m = m_old
        for p in parts:
            m = jnp.maximum(m, p)
        s = row_s[r, :] * jnp.exp2(m_old - m)
        for p in parts:
            s = s + jnp.exp2(p - m)
        row_m[r, :] = m
        row_s[r, :] = s
        v3 = v.reshape(RB // 8, 8, CB)
        m_old = col_m[:, cc]
        m = jnp.maximum(m_old, jnp.max(v3, axis=0))
        col_s[:, cc] = col_s[:, cc] * jnp.exp2(m_old - m) + jnp.sum(jnp.exp2(v3 - m[None]), axis=0)
        col_m[:, cc] = m
        return 0

    lax.fori_loop(0, (rows // RB) * (half // CB), logits_step, 0)

    y_lo = jnp.where(t == 0, y, 3 - y)
    d0 = 8 * y_lo + z - 8 * x - 4 * t - 2 * c
    d1 = 8 * (3 - y_lo) + z - 8 * x - 4 * t - 2 * c
    has0 = jnp.logical_and(d0 >= 0, d0 <= 1)
    has1 = jnp.logical_and(d1 >= 0, d1 <= 1)
    has = jnp.logical_or(has0, has1)
    diag_row = jnp.where(has1, rows_own, 0)
    diag_col = jnp.where(has1, d1, jnp.where(has0, d0, 0)) * rows_own
    eye = lax.broadcasted_iota(jnp.int32, (128, 128), 0) == lax.broadcasted_iota(jnp.int32, (128, 128), 1)

    def put(stats, g, m, s):
        top = jnp.max(m, axis=0, keepdims=True)
        stats[g, 0:1, :] = top
        stats[g, 1:2, :] = jnp.sum(s * jnp.exp2(m - top), axis=0, keepdims=True)

    put(col_st, g_col, col_m[...], col_s[...])
    col_st[g_col, 2:3, :] = jnp.zeros((1, half), jnp.float32)

    @pl.when(has)
    def _():
        def diag_step(i, _):
            r = pl.ds(pl.multiple_of(diag_row + i * 128, 128), 128)
            cc = lanes(diag_col + i * 128, 128)
            col_st[g_col, 2:3, cc] = jnp.sum(jnp.where(eye, logits[r, cc], 0.0), axis=0, keepdims=True)
            return 0
        lax.fori_loop(0, rows_own // 128, diag_step, 0)

    def exchange(buffer, g, peer):
        k = count[0]
        count[0] += 15

        def one(i):
            return pltpu.make_async_remote_copy(
                src_ref=buffer.at[g], dst_ref=buffer.at[g], send_sem=send.at[k + i - 1], recv_sem=recv.at[k],
                device_id=peer(i), device_id_type=MESH,
            )

        def start(i, _):
            one(i).start()
            return 0

        lax.fori_loop(1, 16, start, 0)
        everything = buffer.at[pl.ds(0, 15)]

        def finish_send(i, _):
            one(i).wait_send()
            return 0

        def wait():
            pltpu.make_async_copy(everything, everything, recv.at[k]).wait()
        return wait, lambda: lax.fori_loop(1, 16, finish_send, 0)

    wait_col, sent_col = exchange(col_st, g_col, col_peer)
    put(row_st, g_row, row_m[...].T, row_s[...].T)
    wait_row, sent_row = exchange(row_st, g_row, row_peer)

    def lse_of(stats):
        m = stats[:, 0, :]
        top = jnp.max(m, axis=0, keepdims=True)
        return top + jnp.log2(jnp.sum(stats[:, 1, :] * jnp.exp2(m - top), axis=0, keepdims=True))

    wait_col()
    col_lse = lse_of(col_st)
    col_m[0:1, :] = col_lse
    pos = jnp.sum(col_st[:, 2, :], axis=0, keepdims=True)
    loss_c[g_row] = jnp.full((1, 128), jnp.sum(col_lse - 2.0 * pos), jnp.float32)
    wait_row()
    row_lse = lse_of(row_st)
    loss_r[g_col] = jnp.full((1, 128), jnp.sum(row_lse), jnp.float32)
    row_lse_b[...] = jnp.broadcast_to(row_lse, (128, rows)).T
    wait_lc, sent_lc = exchange(loss_c, g_row, row_peer)
    wait_lr, sent_lr = exchange(loss_r, g_col, col_peer)

    def weights_step(i, _):
        r = pl.ds(pl.multiple_of((i % (rows // RB)) * RB, RB), RB)
        cc = (i // (rows // RB)) * CB
        rl = row_lse_b[r, :]
        for j in range(CB // 128):
            lj = lanes(cc + j * 128, 128)
            v = logits[r, lj]
            w[r, lj] = (jnp.exp2(v - rl) + jnp.exp2(v - col_m[0:1, lj])).astype(jnp.bfloat16)
        return 0

    lax.fori_loop(0, (rows // RB) * (half // CB), weights_step, 0)

    @pl.when(has)
    def _():
        def diag_step(i, _):
            r = pl.ds(pl.multiple_of(diag_row + i * 128, 128), 128)
            cc = lanes(diag_col + i * 128, 128)
            v = logits[r, cc]
            wv = jnp.exp2(v - row_lse_b[r, :]) + jnp.exp2(v - col_m[0:1, cc])
            w[r, cc] = jnp.where(eye, wv - 2.0, wv).astype(jnp.bfloat16)
            return 0
        lax.fori_loop(0, rows_own // 128, diag_step, 0)

    def text_grad(av, c0, n):
        step = 128
        def go(i, _):
            cc = lanes(c0 + i * step, step)
            wv = w[:, cc]
            v = jnp.dot(imgt[av].reshape(dim // 2, rows), wv, preferred_element_type=jnp.float32)
            tg[av, :, :, :, cc] = v.reshape(2, 8, 32, step).astype(SUM_TYPE)
            return 0
        lax.fori_loop(0, n // step, go, 0)

    def up(v):
        return v.astype(jnp.float32)

    def add(dst, at, src):
        dst[at] = (up(dst[at]) + up(src)).astype(dst.dtype)

    def scatter_p(c0, n, n1):
        cc = pl.ds(c0, n)
        halves = {1: (0, n1), -1: (n1, n - n1)}
        from_mate = [
            message(tg.at[1 - a, :, (z + o) % 8, :, cc], land_py.at[j], mate) for j, o in enumerate(OFFSETS_Z)
        ]
        yield
        def add_mate(j):
            from_mate[j].wait_recv()
            add(tg, (a, slice(None), (z + OFFSETS_Z[j]) % 8, slice(None), cc), land_py[j])
        add_mate(0)
        ring = {}
        for d in (1, -1):
            h0, hn = halves[d]
            ring[d] = message(
                tg.at[a, :, (z + 4) % 8, :, pl.ds(c0 + h0, hn)],
                land_pz.at[(1 - d) // 2, 0, :, :, pl.ds(h0, hn)], z_next[d],
            )
        yield
        for s in (2, 3, 4):
            for d in (1, -1):
                o = (8 + d * (5 - s)) % 8
                add_mate(OFFSETS_Z.index(o))
                ring[d].wait_recv()
                h0, hn = halves[d] if s == 2 else (0, n)
                add(tg, (a, slice(None), (z + o) % 8, slice(None), pl.ds(c0 + h0, hn)),
                    land_pz[(1 - d) // 2, s - 2, :, :, h0:h0 + hn])
                ring[d] = message(tg.at[a, :, (z + o) % 8, :, cc], land_pz.at[(1 - d) // 2, s - 1], z_next[d])
                yield
        from_mate[7].wait_recv()
        v = up(tg[a, :, z, :, cc]) + up(land_py[7])
        for d in (1, -1):
            ring[d].wait_recv()
            v = v + up(land_pz[(1 - d) // 2, 3])
        fin[:, :, cc] = v

    def scatter_q(c0, n, n1):
        cc = pl.ds(c0, n)
        halves = {1: (0, n1), -1: (n1, n - n1)}
        ring = {}
        for d in (1, -1):
            h0, hn = halves[d]
            ring[d] = message(
                tg.at[:, :, (z + 4) % 8, :, pl.ds(c0 + h0, hn)],
                land_qz.at[(1 - d) // 2, 0, :, :, :, pl.ds(h0, hn)], z_next[d],
            )
        yield
        for s in (2, 3, 4):
            for d in (1, -1):
                o = (8 + d * (5 - s)) % 8
                ring[d].wait_recv()
                h0, hn = halves[d] if s == 2 else (0, n)
                add(tg, (slice(None), slice(None), (z + o) % 8, slice(None), pl.ds(c0 + h0, hn)),
                    land_qz[(1 - d) // 2, s - 2, :, :, :, h0:h0 + hn])
                ring[d] = message(tg.at[:, :, (z + o) % 8, :, cc], land_qz.at[(1 - d) // 2, s - 1], z_next[d])
                yield
        for d in (1, -1):
            ring[d].wait_recv()
        v = up(tg[1 - a, :, z, :, cc]) + up(land_qz[0, 3, 1 - a]) + up(land_qz[1, 3, 1 - a])
        tg[1 - a, :, z, :, cc] = v.astype(SUM_TYPE)
        last = message(tg.at[1 - a, :, z, :, cc], land_qy, mate)
        v = up(tg[a, :, z, :, cc]) + up(land_qz[0, 3, a]) + up(land_qz[1, 3, a])
        yield
        last.wait_recv()
        fin[:, :, cc] = v + up(land_qy[...])

    def image_grad(xv):
        s = slot_of(xv, t)
        def go(i, _):
            r = pl.ds(pl.multiple_of(i * RB, RB), RB)
            tv = txt[s // 2, s % 2].reshape(256, half)
            v = lax.dot_general(w[r, :], tv, (((1,), (1,)), ((), ())), preferred_element_type=jnp.float32)
            ig[s, 0, r, :] = v[:, :128].astype(SUM_TYPE)
            ig[s, 1, r, :] = v[:, 128:].astype(SUM_TYPE)
            return 0
        lax.fori_loop(0, rows // RB, go, 0)

    def scatter_img():
        cores = {}
        for o in OFFSETS_X:
            xv = (x + o) % 4
            image_grad(xv)
            cores[o] = message(ig.at[slot_of(xv, t), 1 - c], land_c.at[o], core_mate)
            yield
        def add_core(o):
            cores[o].wait_recv()
            add(ig, (slot_of((x + o) % 4, t), c), land_c[o])
        add_core(2)
        so = slot_of((x + 2) % 4, t)
        first = {}
        for d, b in ((1, t), (-1, 1 - t)):
            first[d] = message(ig.at[so, c, block(b)], land_x1.at[(1 - d) // 2], x_next[d])
        yield
        second = []
        for d, o, b in ((1, 1, t), (-1, 3, 1 - t)):
            s = slot_of((x + o) % 4, t)
            add_core(o)
            second.append(message(
                ig.at[s, c, block(1 - b)], land_x2.at[(1 - d) // 2, block(1 - b)], x_next[d]))
            yield
            first[d].wait_recv()
            add(ig, (s, c, block(b)), land_x1[(1 - d) // 2])
            second.append(message(ig.at[s, c, block(b)], land_x2.at[(1 - d) // 2, block(b)], x_next[d]))
            yield
        cores[0].wait_recv()
        for copy in second:
            copy.wait_recv()
        s = slot_of(x, t)

        def total(b):
            v = up(ig[s, c, block(b)]) + up(land_c[0, block(b)])
            return v + up(land_x2[0, block(b)]) + up(land_x2[1, block(b)])

        land_xp[0] = total(1 - t)
        last = message(land_xp.at[0], land_xp.at[1], partner)
        mine = total(t)
        land_xp[2] = mine
        yield
        last.wait_recv()
        img_out[...] = (land_xp[2] + land_xp[1]) * factor

    (cp, np_, np1, _), (cq, nq, nq1, _) = PARTS
    text_grad(1 - a, cp, np_)
    p_stream = scatter_p(cp, np_, np1)
    next(p_stream)
    text_grad(a, cq, nq)
    text_grad(1 - a, cq, nq)
    q_stream = scatter_q(cq, nq, nq1)
    next(q_stream)
    text_grad(a, cp, np_)
    i_stream = scatter_img()
    interleave(p_stream, q_stream, i_stream)

    k = count[0]
    count[0] += 3
    out_near = pltpu.make_async_remote_copy(
        src_ref=fin.at[0], dst_ref=land_o.at[c], send_sem=send.at[k], recv_sem=recv.at[k],
        device_id=core_mate, device_id_type=MESH,
    )
    in_near = pltpu.make_async_remote_copy(
        src_ref=fin.at[0], dst_ref=land_o.at[1 - c], send_sem=send.at[k], recv_sem=recv.at[k],
        device_id=core_mate, device_id_type=MESH,
    )
    out_far = pltpu.make_async_remote_copy(
        src_ref=fin.at[1], dst_ref=land_o.at[c], send_sem=send.at[k + 1], recv_sem=recv.at[k + 1 + c],
        device_id=dev(dy=y_part, dc=t), device_id_type=MESH,
    )
    in_far = [
        pltpu.make_async_remote_copy(
            src_ref=fin.at[1], dst_ref=land_o.at[q], send_sem=send.at[k + 1], recv_sem=recv.at[k + 1 + q],
            device_id=partner, device_id_type=MESH,
        )
        for q in range(2)
    ]
    out_far.start()

    @pl.when(same)
    def _():
        land_o[c] = fin[0]
        in_near.wait_recv()

    @pl.when(jnp.logical_not(same))
    def _():
        out_near.start()
        in_far[0].wait_recv()
        in_far[1].wait_recv()

    txt_out[:, :half] = land_o[0] * factor
    txt_out[:, half:] = land_o[1] * factor

    wait_lc()
    wait_lr()
    total = jnp.sum(loss_c[...], axis=0) + jnp.sum(loss_r[...], axis=0)
    loss_out[...] = total * (1.0 / (LOG2E * 2.0 * batch))

    out_far.wait_send()

    @pl.when(same)
    def _():
        swap_own.wait_send()

    @pl.when(jnp.logical_not(same))
    def _():
        swap_far[0].wait_send()
        swap_far[1].wait_send()
        out_near.wait_send()

    for copy in unsent:
        copy.wait_send()
    sent_col()
    sent_row()
    sent_lc()
    sent_lr()


def shards(image_rows, text_rows):
    rows_own, feat_own = image_rows.shape
    txt_t = text_rows.T
    cols = txt_t.shape[1]
    half = cols // 2
    rows = 2 * rows_own
    dim = 8 * feat_own
    (_, np_, _, _), (_, nq, _, _) = PARTS
    f32, bf16 = jnp.float32, jnp.bfloat16
    vmem = pltpu.VMEM
    n_sem = 200
    scratch = [
        vmem((rows, dim), bf16),
        vmem((2, 2, 256, rows), bf16),
        vmem((2, 2, 8, 32, half), bf16),
        vmem((rows, half), f32),
        vmem((rows, half), bf16),
        vmem((2, 2, 8, 32, half), SUM_TYPE),
        vmem((4, 2, rows, 128), SUM_TYPE),
        vmem((rows, 128), f32),
        vmem((rows, 128), f32),
        vmem((8, half), f32),
        vmem((8, half), f32),
        vmem((16, 2, rows), f32),
        vmem((16, 3, half), f32),
        vmem((rows, 128), f32),
        vmem((16, 1, 128), f32),
        vmem((16, 1, 128), f32),
        vmem((8, 2, 32, np_), SUM_TYPE),
        vmem((2, 4, 2, 32, np_), SUM_TYPE),
        vmem((2, 4, 2, 2, 32, nq), SUM_TYPE),
        vmem((2, 32, nq), SUM_TYPE),
        vmem((4, rows, 128), SUM_TYPE),
        vmem((2, rows_own, 128), SUM_TYPE),
        vmem((2, rows, 128), SUM_TYPE),
        vmem((3, rows_own, 128), f32),
        vmem((2, 32, half), f32),
        vmem((2, 32, half), f32),
        pltpu.SemaphoreType.DMA((n_sem,)),
        pltpu.SemaphoreType.DMA((n_sem,)),
        pltpu.SemaphoreType.DMA((2,)),
    ]
    loss, img_grad, txt_grad = pl.pallas_call(
        kernel,
        out_shape=(
            jax.ShapeDtypeStruct((1, 128), f32),
            jax.ShapeDtypeStruct((rows_own, feat_own), f32),
            jax.ShapeDtypeStruct((32, cols), f32),
        ),
        in_specs=[pl.BlockSpec(memory_space=pl.ANY)] * 2,
        out_specs=[pl.BlockSpec(memory_space=pltpu.VMEM)] * 3,
        scratch_shapes=scratch,
        compiler_params=pltpu.CompilerParams(
            collective_id=0, has_side_effects=True, vmem_limit_bytes=61 * 1024 * 1024,
        ),
    )(image_rows, txt_t)
    return loss[0, 0], img_grad, txt_grad.T


def solution(mesh):
    return jax.shard_map(
        shards,
        mesh=mesh,
        in_specs=(P("row", "col"), P("col", "row")),
        out_specs=(P(), P("row", "col"), P("col", "row")),
        check_vma=False,
    )
```

time: 757 us -> 174 us (0.23)
  blocking collectives: 375 us -> 0 us
  waiting for transfers between devices: 308 us -> 0 us
  Pallas kernels: 0 us -> 169 us
  matrix products: 28.8 us -> 0 us
  other arithmetic: 23.7 us -> 0 us
  between operations: 16.9 us -> 1.82 us
    psum x3 -> x0, blocking collectives: 236 us -> none  [the longest x1 138 us: shards(): lax.psum((jnp.sum(jnp.exp(logits - col_top[None, :]), axis=0), col_pos_lo...]
    reduce_scatter x2 -> x0, waiting for transfers between devices: 185 us -> none  [the longest x1 185 us: shards(): lax.psum_scatter(caption_addend, 'row', scatter_dimension=1, tiled=True)]
    pallas_call x0 -> x1, Pallas kernels: none -> 169 us  [shards(): pl.pallas_call(kernel, out_shape=(jax.ShapeDtypeStruct((1, 128), f32), ja...]
    pmax x2 -> x0, blocking collectives: 138 us -> none  [the longest x1 128 us: shards(): col_top = lax.pmax(jnp.max(logits, axis=0), 'row')]
    all_gather x2 -> x0, waiting for transfers between devices: 122 us -> none  [the longest x1 91.1 us: shards(): text_block = lax.all_gather(text_rows, 'row', axis=1, tiled=True)]
    dot_general x3 -> x0, matrix products: 28.8 us -> none  [the longest x1 10.4 us: shards(): jnp.dot(weights.T, image_block, preferred_element_type=jnp.float32)]
    reduce_sum x4 -> x0, other arithmetic: 13.4 us -> none  [the longest x1 6.99 us: shards(): col_pos_local = jnp.sum(masked, axis=0)]
  transfers between devices with their start and end apart: 4 -> 0, of which waited for: 3 -> 0; matrix products, arithmetic and copies ran while one was open for 2% -> 0% of each run, Pallas kernels for 0% -> 0%
where the time goes in v1:
time: 174 us
  Pallas kernels  169 us (97%)
  local copies, waits for them, and re-layouts  3.23 us (2%)
  between operations  1.82 us (1%)
    pallas_call x1, Pallas kernels, shards(): pl.pallas_call(kernel, out_shape=(jax.ShapeDtypeStruct((1, 128), f32), ja...  169 us

profile of v1, /device:TPU:30, one launch (start us, length us, event | category | flops | bytes accessed | tf_op | source)
XLA Modules:
  0.0 173.7 jit_solution(5115884800379621943)
XLA Ops:
  0.6 168.6 %shard_map.49 = (f32[1,128]{1,0:T(1,128)}, f32[768,128]{1,0:T(8,128)}, f32[32,3072]{1,0:T(8,128)}) custom-call(bf16[768,128]{1,0:T(8,128)(2,1)} %img_raw.1, bf16[32,3072]{1,0:T(8,128)(2,1)} %bitcast.5), custom_call_target="tpu_custom_call" | custom-call | tf_op jit(solution)/shard_map/pallas_call | solution.py:639
  169.3 0.0 copy-start.1
  169.3 0.7 copy-done.1
  170.0 0.0 copy-start
  170.0 1.8 %copy.9 = f32[768,128]{1,0:T(8,128)} copy(f32[768,128]{1,0:T(8,128)} %get-tuple-element.13) | data formatting | bytes 786432
  171.8 0.0 copy-done
  171.8 0.7 copy.10
Async XLA Ops:
  169.3 0.7 copy-start.1
  170.0 1.8 %copy-start = (f32[32,3072]{1,0:T(8,128)S(1)}, f32[32,3072]{1,0:T(8,128)}, u32[]{:S(2)}) copy-start(f32[32,3072]{1,0:T(8,128)} %get-tuple-element.8) | copy-start | bytes 1179652
